TPU v7x, 256 devices: a whole 4x4x8 slice. The times are simulated.
256 devices in a mesh: dp: 8 (over y_lo, x), axial: 32 (over y_hi, z, core).
Axes of the slice: x: 4, y: 4 (y_hi: 2, y_lo: 2; y = y_hi * 2 + y_lo), z: 8, core: 2. Of those that a mesh axis runs over, the one named last changes fastest.
Arguments:
- pair_act: bfloat16 [2048, 256, 128], P(('dp', 'axial')), parts along dimension 0, may hold values from -6 to 6
- norm_gain: float32 [128], replicated, may hold values from 0.25 to 1.75
- norm_offset: float32 [128], replicated, may hold values from -3 to 3
- w_query: bfloat16 [128, 128], replicated, may hold values from -0.5 to 0.5
- w_key: bfloat16 [128, 128], replicated, may hold values from -0.5 to 0.5
- w_value: bfloat16 [128, 128], replicated, may hold values from -0.5 to 0.5
- w_bias: bfloat16 [128, 4], replicated, as said below
- w_gate: bfloat16 [128, 128], replicated, may hold values from -0.5 to 0.5
- gate_bias: float32 [128], replicated, may hold values from -4 to 4
- w_out: bfloat16 [128, 128], replicated, may hold values from -0.5 to 0.5
- out_bias: float32 [128], replicated, may hold values from -3 to 3
Outputs:
- pair_update: bfloat16 [2048, 256, 128], P(('dp', 'axial')), parts along dimension 0
There are 8 independent parts, one for each index of `dp`. A program takes and returns all parts, laid end to end along the dimension named above; an argument that names none is the same for every part. Nothing has to cross between parts.
Inputs may be any that keep to these rules, and one draw needn't show every extreme that they name: `w_bias`: normal entries scaled by s / sqrt(128), with s between 1.5 and 50.
All inputs are finite; a program needn't handle non-finite values.
Results may differ from a plain program's by a relative error of at most 0.0024.
The roundings to bfloat16 on the way count: a program that leaves them out, or rounds other values in their place, can miss the bound.
Values may be sent and summed in bfloat16 or wider, within the bound.
A program may use at most 192 MiB of HBM per device.

v0:
```python
import jax
import jax.numpy as jnp
from jax import lax
from jax.sharding import PartitionSpec as P


def normalize(pair_act, norm_gain, norm_offset):
    values_f = pair_act.astype(jnp.float32)
    average = jnp.mean(values_f, axis=-1, keepdims=True)
    spread = jnp.mean((values_f - average) ** 2, axis=-1, keepdims=True)
    scaled = (values_f - average) * lax.rsqrt(spread + 1e-05) * norm_gain + norm_offset
    return scaled.astype(jnp.bfloat16)


def project(normed, weight):
    flat = normed.reshape(-1, normed.shape[-1])
    return jnp.dot(flat, weight, preferred_element_type=jnp.float32).reshape(
        normed.shape[:-1] + (weight.shape[1],)
    )


def bias_layout(normed, w_bias):
    return jnp.einsum("kic,ch->khi", normed, w_bias, preferred_element_type=jnp.float32).astype(
        jnp.bfloat16
    )


def split_heads(tensor, heads):
    return tensor.reshape(tensor.shape[:-1] + (heads, tensor.shape[-1] // heads))


def on_device(
    pair_act,
    norm_gain,
    norm_offset,
    w_query,
    w_key,
    w_value,
    w_bias,
    w_gate,
    gate_bias,
    w_out,
    out_bias,
):
    row_count, count, width = pair_act.shape
    heads = w_bias.shape[1]
    head_size = width // heads
    normed = normalize(pair_act, norm_gain, norm_offset)
    bias_rows = bias_layout(normed, w_bias)
    columns = lax.all_to_all(normed, "axial", split_axis=1, concat_axis=0, tiled=True)
    queries = split_heads(
        (project(columns, w_query) * (1.0 / head_size**0.5)).astype(jnp.bfloat16), heads
    )
    key_rows = split_heads(project(columns, w_key).astype(jnp.bfloat16), heads)
    value_rows = split_heads(project(columns, w_value).astype(jnp.bfloat16), heads)
    gating = jax.nn.sigmoid(project(columns, w_gate) + gate_bias)
    bias_whole = lax.all_gather(bias_rows, "axial", axis=0, tiled=True)
    scores = jnp.einsum("ijhc,kjhc->ijkh", queries, key_rows, preferred_element_type=jnp.float32)
    scores = scores + jnp.transpose(bias_whole.astype(jnp.float32), (2, 0, 1))[:, None, :, :]
    highest = jnp.max(scores, axis=2, keepdims=True)
    expo = jnp.exp(scores - highest)
    running_sum = jnp.sum(expo, axis=2)
    weights = expo.astype(jnp.bfloat16)
    summed = jnp.einsum("ijkh,kjhc->ijhc", weights, value_rows, preferred_element_type=jnp.float32)
    attended = (summed / running_sum[..., None]).reshape(columns.shape)
    gated = (gating * attended).astype(jnp.bfloat16)
    update_cols = (project(gated, w_out) + out_bias).astype(jnp.bfloat16)
    return lax.all_to_all(update_cols, "axial", split_axis=0, concat_axis=1, tiled=True)


def solution(mesh):
    return jax.shard_map(
        on_device,
        mesh=mesh,
        in_specs=(P(("dp", "axial"), None, None), P(), P(), P(), P(), P(), P(), P(), P(), P(), P()),
        out_specs=P(("dp", "axial"), None, None),
        check_vma=False,
    )
```

profile of v0, /device:TPU:1, one launch (start us, length us, event | category | flops | bytes accessed | tf_op | source)
XLA Modules:
  0.0 96.8 jit_solution(2114301833350053437)
XLA Ops:
  0.0 0.0 copy-start
  0.0 0.0 copy-start.1
  0.0 0.0 copy-start.2
  0.0 1.5 %convert_reduce_fusion = f32[8,256]{0,1:T(8,128)S(1)} fusion(bf16[8,256,128]{2,1,0:T(8,128)(2,1)} %param.11), kind=kLoop, calls=%fused_computation.18 | loop fusion | flops 522240 | bytes 532480 | tf_op jit(solution)/shard_map/reduce_sum | solution.py:9
  1.5 1.7 %fusion.23 = f32[8,256]{0,1:T(8,128)S(1)} fusion(f32[8,256]{0,1:T(8,128)S(1)} %broadcast_multiply_fusion, bf16[8,256,128]{2,1,0:T(8,128)(2,1)} %param.11), kind=kLoop, calls=%fused_computation.27 | loop fusion | flops 1046528 | bytes 540672 | tf_op jit(solution)/shard_map/reduce_sum | solution.py:10
  3.3 2.4 %fusion.26 = bf16[8,256,128]{2,0,1:T(8,128)(2,1)} fusion(f32[128]{0:T(128)} %param.13, f32[128]{0:T(128)} %param.12, f32[8,256]{0,1:T(8,128)S(1)} %add_rsqrt_fusion, f32[8,256]{0,1:T(8,128)S(1)} %broadcast_multiply_fusion, bf16[8,256,128]{2,1,0:T(8,128)(2,1)} %param.11), kind=kLoop, calls=%fused_computation.30 | loop fusion | flops 1572864 | bytes 1065984 | tf_op jit(solution)/shard_map/convert_element_type | solution.py:12
  5.7 12.8 %all-to-all-start = ((bf16[8,256,128]{2,0,1:T(8,128)(2,1)}), bf16[8,256,128]{2,0,1:T(8,128)(2,1)S(1)}, u32[]{:S(2)}, u32[]{:S(2)}) async-start(bf16[8,256,128]{2,0,1:T(8,128)(2,1)} %fusion.26), calls=%async_computation | async-start | bytes 1048576 | tf_op jit(solution)/shard_map/all_to_all | solution.py:50
  18.4 3.5 %fusion.45 = bf16[8,256,4]{0,2,1:T(4,128)(2,1)S(1)} fusion(bf16[8,256,128]{2,0,1:T(8,128)(2,1)} %fusion.26, bf16[128,4]{0,1:T(4,128)(2,1)} %param.17), kind=kOutput, calls=%fused_computation.51 | convolution fusion | flops 2097152 | bytes 541696 | tf_op jit(solution)/shard_map/kic,ch->khi/dot_general | solution.py:23
  21.9 0.2 copy.35
  22.1 45.6 %all_gather.3 = bf16[256,4,256]{2,1,0:T(4,128)(2,1)S(1)} all-gather(bf16[8,4,256]{2,1,0:T(4,128)(2,1)S(1)} %bitcast.79), channel_id=1, replica_groups=mesh['dp'=8,'axial'=32] {'axial'}, dimensions={0}, use_global_device_ids=true | all-gather | bytes 540672 | tf_op jit(solution)/shard_map/all_gather | solution.py:57
  67.6 0.1 convert_bitcast_fusion
  67.8 0.2 copy.26
  68.0 0.0 all-to-all-done
  68.0 0.0 copy-done
  68.0 0.3 fusion.15
  68.3 0.0 copy-done.1
  68.3 0.3 convolution_convert_fusion
  68.7 0.0 copy-done.2
  68.7 0.3 convolution_convert_fusion.1
  69.1 1.3 %fusion = (f32[256,8,4]{0,2,1:T(4,128)S(1)}, f32[8,4,256,256]{3,2,1,0:T(8,128)S(1)}) fusion(f32[256,256,4]{0,1,2:T(8,128)S(1)} %copy.26, bf16[256,8,4,32]{0,3,2,1:T(8,128)(2,1)S(1)} %bitcast.76, bf16[256,8,4,32]{0,3,2,1:T(8,128)(2,1)S(1)} %bitcast.75), kind=kOutput, calls=%fused_computation.2 | convolution fusion | flops 138403840 | bytes 10518528 | tf_op jit(solution)/shard_map/ijhc,kjhc->ijkh/dot_general | solution.py:58
  70.4 1.5 %fusion.1 = f32[256,8,4]{0,2,1:T(4,128)S(1)} fusion(f32[8,4,256,256]{3,2,1,0:T(8,128)S(1)} %get-tuple-element.6, f32[256,8,4]{0,2,1:T(4,128)S(1)} %get-tuple-element.5, f32[256,256,4]{0,1,2:T(8,128)S(1)} %copy.26), kind=kLoop, calls=%fused_computation.3 | loop fusion | flops 6283264 | bytes 9502720 | tf_op jit(solution)/shard_map/reduce_sum | solution.py:62
  71.9 0.0 copy-start.3
  71.9 0.0 copy-start.4
  71.9 0.0 copy-start.5
  71.9 0.0 copy-start.6
  72.0 1.7 %fusion.20 = f32[256,8,4,32]{0,3,2,1:T(8,128)S(1)} fusion(bf16[256,8,4,32]{0,3,2,1:T(8,128)(2,1)S(1)} %bitcast.78, f32[8,4,256,256]{3,2,1,0:T(8,128)S(1)} %get-tuple-element.6, f32[256,8,4]{0,2,1:T(4,128)S(1)} %get-tuple-element.5, f32[256,256,4]{0,1,2:T(8,128)S(1)} %copy.26, f32[256,8,4]{0,2,1:T(4,128)S(1)} %fusion.1), kind=kOutput, calls=%fused_computation.26 | convolution fusion | flops 140771328 | bytes 11075584 | tf_op jit(solution)/shard_map/ijkh,kjhc->ijhc/dot_general | solution.py:64
  73.6 0.3 copy.28
  73.9 0.0 copy-done.3
  74.0 0.0 copy-done.4
  74.0 0.0 copy-done.5
  74.0 0.0 copy-done.6
  74.0 0.5 fusion.16
  74.5 0.3 copy.29
  74.9 21.0 %all_to_all.33 = bf16[256,8,128]{2,1,0:T(8,128)(2,1)S(1)} all-to-all(bf16[256,8,128]{2,1,0:T(8,128)(2,1)S(1)} %copy.29), channel_id=1, replica_groups=mesh['dp'=8,'axial'=32] {'axial'}, dimensions={0} | all-to-all | bytes 1048576 | tf_op jit(solution)/shard_map/all_to_all | solution.py:68
  95.9 0.9 copy.61
  (2 shorter events, 0.0 us)
Async XLA Ops:
  0.0 68.0 %copy-start = (bf16[128,128]{1,0:T(8,128)(2,1)S(1)}, bf16[128,128]{1,0:T(8,128)(2,1)}, u32[]{:S(2)}) copy-start(bf16[128,128]{1,0:T(8,128)(2,1)} %param.14) | copy-start | bytes 98308
  0.0 68.3 %copy-start.1 = (bf16[128,128]{1,0:T(8,128)(2,1)S(1)}, bf16[128,128]{1,0:T(8,128)(2,1)}, u32[]{:S(2)}) copy-start(bf16[128,128]{1,0:T(8,128)(2,1)} %param.15) | copy-start | bytes 98308
  0.0 68.7 %copy-start.2 = (bf16[128,128]{1,0:T(8,128)(2,1)S(1)}, bf16[128,128]{1,0:T(8,128)(2,1)}, u32[]{:S(2)}) copy-start(bf16[128,128]{1,0:T(8,128)(2,1)} %param.16) | copy-start | bytes 98308
  5.7 62.3 %all-to-all-start = ((bf16[8,256,128]{2,0,1:T(8,128)(2,1)}), bf16[8,256,128]{2,0,1:T(8,128)(2,1)S(1)}, u32[]{:S(2)}, u32[]{:S(2)}) async-start(bf16[8,256,128]{2,0,1:T(8,128)(2,1)} %fusion.26), calls=%async_computation | async-start | bytes 1048576 | tf_op jit(solution)/shard_map/all_to_all | solution.py:50
  71.9 2.0 %copy-start.3 = (bf16[128,128]{1,0:T(8,128)(2,1)S(1)}, bf16[128,128]{1,0:T(8,128)(2,1)}, u32[]{:S(2)}) copy-start(bf16[128,128]{1,0:T(8,128)(2,1)} %param.20) | copy-start | bytes 98308
  71.9 2.0 %copy-start.4 = (bf16[128,128]{1,0:T(8,128)(2,1)S(1)}, bf16[128,128]{1,0:T(8,128)(2,1)}, u32[]{:S(2)}) copy-start(bf16[128,128]{1,0:T(8,128)(2,1)} %param.18) | copy-start | bytes 98308
  71.9 2.0 %copy-start.5 = (f32[128]{0:T(128)S(1)}, f32[128]{0:T(128)}, u32[]{:S(2)}) copy-start(f32[128]{0:T(128)} %param.21) | copy-start | bytes 1540
  71.9 2.0 %copy-start.6 = (f32[128]{0:T(128)S(1)}, f32[128]{0:T(128)}, u32[]{:S(2)}) copy-start(f32[128]{0:T(128)} %param.19) | copy-start | bytes 1540
where the time goes:
time: 97.7 us; the launch traced here: 96.8 us
  blocking collectives  66.6 us (68%)
  starting transfers between devices  12.8 us (13%)
  matrix products  8.01 us (8%)
  other arithmetic  7.29 us (7%)
  local copies, waits for them, and re-layouts  1.97 us (2%)
    all_gather x1, blocking collectives, on_device(): bias_whole = lax.all_gather(bias_rows, 'axial', axis=0, tiled=True)  45.6 us
    all_to_all x1, blocking collectives, on_device(): lax.all_to_all(update_cols, 'axial', split_axis=0, concat_axis=1, tiled=T...  21 us
    all_to_all x1, starting transfers between devices, on_device(): lax.all_to_all(normed, 'axial', split_axis=1, concat_axis=0, tiled=True)  12.8 us
    dot_general x1, matrix products, bias_layout(): jnp.einsum('kic,ch->khi', normed, w_bias, preferred_element_type=jnp.floa...  3.46 us
    convert_element_type x1, other arithmetic, normalize(): return scaled.astype(jnp.bfloat16)  2.38 us
  transfers between devices with their start and end apart: 1, of which 0 were waited for; matrix products, arithmetic and copies ran while one was open for 4% of the time, Pallas kernels for 0%

commit v1 on v0

v1 whole, which is shorter than its diff:
```python
import functools

import jax
import jax.numpy as jnp
from jax import lax
from jax.experimental import pallas as pl
from jax.experimental.pallas import tpu as pltpu
from jax.sharding import PartitionSpec as P

MESH = pl.DeviceIdType.MESH
NZ, NY, NCORE = 8, 2, 2
N = NZ * NY * NCORE
ROWS = 8
RES = 256
C = 128
H = 4
DH = 32
CHUNKS = 2
COLS = RES // N // CHUNKS
MSG = COLS * ROWS

OFFSETS = [(dz, dy, dc) for dz in range(NZ) for dy in range(NY) for dc in range(NCORE)][1:]

NT = (((1,), (1,)), ((), ()))


def dot_nt(a, b):
    return lax.dot_general(a, b, NT, preferred_element_type=jnp.float32)


def dot_nn(a, b):
    return jnp.dot(a, b, preferred_element_type=jnp.float32)


def kernel(
    x_hbm, gain_hbm, offset_hbm, wq_hbm, wk_hbm, wv_hbm, wb_hbm, wg_hbm, gb_hbm, wo_hbm, ob_hbm,
    out_ref,
    x_v, gain_v, offset_v, wq_v, wk_v, wv_v, wb_v, wg_v, gb_v, wo_v, ob_v,
    send1, recv1, send2, bias_all, bias_f, w_t, gate_bias_t,
    load_sem, s1_sem, r1_sem, s2_sem, r2_sem, bs_sem, br_sem,
):
    me = lax.axis_index("axial")
    my_y, my_z, my_c = me // (NZ * NCORE), (me // NCORE) % NZ, me % NCORE

    def other(dz, dy, dc):
        return ((my_y + dy) % NY) * (NZ * NCORE) + ((my_z + dz) % NZ) * NCORE + (my_c + dc) % NCORE

    loads = []
    for n, (src, dst) in enumerate(
        [
            (x_hbm, x_v), (gain_hbm, gain_v), (offset_hbm, offset_v), (wb_hbm, wb_v), (wq_hbm, wq_v), (wk_hbm, wk_v),
            (wv_hbm, wv_v), (wg_hbm, wg_v), (gb_hbm, gb_v), (wo_hbm, wo_v), (ob_hbm, ob_v),
        ]
    ):
        copy = pltpu.make_async_copy(src, dst, load_sem.at[n])
        copy.start()
        loads.append(copy)

    barrier = pltpu.get_barrier_semaphore()
    for off in OFFSETS:
        pl.semaphore_signal(barrier, inc=1, device_id={"axial": other(*off)}, device_id_type=MESH)

    for n in range(4):
        loads[n].wait()

    gain = gain_v[...][None]
    shift = offset_v[...][None]
    wb = wb_v[...].astype(jnp.float32)
    wb_rep = jnp.broadcast_to(wb[:, None, :], (H, ROWS, C)).reshape(H * ROWS, C)
    row_of = lax.broadcasted_iota(jnp.int32, (H * ROWS, C), 0) % ROWS
    wb_row = [jnp.where(row_of == r, wb_rep, 0.0).astype(jnp.bfloat16) for r in range(ROWS)]

    STEP = 32
    for block in range(RES // STEP):
        values = x_v[:, pl.ds(block * STEP, STEP), :].astype(jnp.float32)
        average = jnp.mean(values, axis=-1, keepdims=True)
        centred = values - average
        spread = jnp.mean(centred * centred, axis=-1, keepdims=True)
        scaled = centred * lax.rsqrt(spread + 1e-05) * gain + shift
        turned = jnp.swapaxes(scaled, 0, 1).reshape(STEP // 2, 2 * ROWS, C)
        turned = turned.astype(jnp.bfloat16).reshape(STEP * ROWS // MSG, MSG, C)
        first = block * STEP * ROWS // MSG
        send1[pl.ds(first, STEP * ROWS // MSG)] = turned
        x_v[:, pl.ds(block * STEP, STEP), :] = scaled.astype(jnp.bfloat16)

    acc = dot_nt(wb_row[0], x_v[0])
    for r in range(1, ROWS):
        acc = acc + dot_nt(wb_row[r], x_v[r])
    bias_all[my_y, my_z, my_c] = acc.astype(jnp.bfloat16)

    pl.semaphore_wait(barrier, N - 1)

    bias_sends = []

    def bias_send(src, k, n, off):
        copy = pltpu.make_async_remote_copy(
            src_ref=src, dst_ref=src, send_sem=bs_sem.at[k], recv_sem=br_sem.at[n],
            device_id={"axial": other(*off)}, device_id_type=MESH,
        )
        copy.start()
        bias_sends.append(copy)

    def bias_wait(ref, n):
        pltpu.make_async_copy(ref, ref, br_sem.at[n]).wait()

    for dz in range(1, NZ):
        bias_send(bias_all.at[my_y, my_z, my_c], dz - 1, 0, (dz, 0, 0))

    def exchange(c, src, dst, send_sem, recv_sem):
        for off in OFFSETS:
            to = other(*off)
            pltpu.make_async_remote_copy(
                src_ref=src.at[c * N + to], dst_ref=dst.at[c * N + me], send_sem=send_sem.at[c], recv_sem=recv_sem.at[c],
                device_id={"axial": to}, device_id_type=MESH,
            ).start()
        dst[c * N + me] = src[c * N + me]

    def arrived(c, ref, sem):
        part = ref.at[pl.ds(c * N, N - 1)]
        pltpu.make_async_copy(part, part, sem.at[c]).wait()

    exchange(0, send1, recv1, s1_sem, r1_sem)

    for n in range(4, len(loads)):
        loads[n].wait()
    w_t[0:C] = wq_v[...].astype(jnp.float32).T.astype(jnp.bfloat16)
    w_t[C : 2 * C] = wv_v[...].astype(jnp.float32).T.astype(jnp.bfloat16)
    w_t[2 * C : 3 * C] = wg_v[...].astype(jnp.float32).T.astype(jnp.bfloat16)
    gate_bias_t[...] = jnp.broadcast_to(gb_v[...], (C, C)).T

    bias_wait(bias_all.at[my_y, pl.ds(0, NZ - 1), my_c], 0)
    mine = bias_all.at[my_y, :, my_c]
    bias_send(mine, 7, 1, (0, 1, 0))
    bias_send(mine, 8, 2, (0, 0, 1))
    for c in range(1, CHUNKS):
        exchange(c, send1, recv1, s1_sem, r1_sem)
    bias_wait(mine, 1)
    bias_send(bias_all.at[1 - my_y, :, my_c], 9, 3, (0, 0, 1))
    bias_wait(mine, 2)
    bias_wait(mine, 3)
    for h in range(H):
        part = bias_all[:, :, :, h * ROWS : (h + 1) * ROWS, :]
        bias_f[h] = part.astype(jnp.float32).reshape(RES, RES)

    lane_head = lax.broadcasted_iota(jnp.int32, (RES, C), 1) // DH
    scale = 1.0 / DH**0.5

    def column(x_j):
        key_rows = dot_nn(x_j, wk_v[...])
        turned = dot_nt(w_t[...], x_j)
        queries = (turned[0:C] * scale).astype(jnp.bfloat16)
        values = turned[C : 2 * C].astype(jnp.bfloat16)
        gate_bias = gate_bias_t[...]
        gating = jax.nn.sigmoid(turned[2 * C :] + jnp.concatenate([gate_bias, gate_bias], axis=1))
        outs = []
        for h in range(H):
            key_h = jnp.where(lane_head == h, key_rows, 0.0).astype(jnp.bfloat16)
            scores = dot_nn(key_h, queries) + bias_f[h]
            highest = jnp.max(scores, axis=0, keepdims=True)
            expo = jnp.exp(scores - highest)
            total = jnp.sum(expo, axis=0, keepdims=True)
            summed = dot_nn(values[h * DH : (h + 1) * DH], expo.astype(jnp.bfloat16))
            outs.append(summed / total)
        attended = jnp.concatenate(outs, axis=0)
        gated = (gating * attended).T.astype(jnp.bfloat16)
        return dot_nn(gated, wo_v[...]) + ob_v[...]

    for c in range(CHUNKS):
        arrived(c, recv1, r1_sem)

        def pair(p, carry, c=c):
            rows = pl.ds(pl.multiple_of(p * 2 * ROWS, 2 * ROWS), 2 * ROWS)
            both = recv1[pl.ds(c * N, N), rows, :].astype(jnp.float32).reshape(N, 2, ROWS, C)
            done = [column(both[:, q].reshape(RES, C).astype(jnp.bfloat16)).reshape(N, ROWS, C) for q in range(2)]
            send2[pl.ds(c * N, N), rows, :] = jnp.concatenate(done, axis=1).astype(jnp.bfloat16)
            return carry

        lax.fori_loop(0, COLS // 2, pair, 0)
        exchange(c, send2, out_ref, s2_sem, r2_sem)

    for c in range(CHUNKS):
        arrived(c, out_ref, r2_sem)
    for copy in bias_sends:
        copy.wait_send()
    for c in range(CHUNKS):
        arrived(c, send1, s1_sem)
        arrived(c, send2, s2_sem)


def on_device(x, gain, shift, wq, wk, wv, wb, wg, gb, wo, ob):
    blocks = jax.ShapeDtypeStruct((CHUNKS * N, MSG, C), jnp.bfloat16)
    bf16, f32 = jnp.bfloat16, jnp.float32
    out = pl.pallas_call(
        kernel,
        out_shape=blocks,
        in_specs=[pl.BlockSpec(memory_space=pltpu.HBM)] * 11,
        out_specs=pl.BlockSpec(memory_space=pltpu.VMEM),
        scratch_shapes=[
            pltpu.VMEM((ROWS, RES, C), bf16),
            pltpu.VMEM((1, C), f32),
            pltpu.VMEM((1, C), f32),
            pltpu.VMEM((C, C), bf16),
            pltpu.VMEM((C, C), bf16),
            pltpu.VMEM((C, C), bf16),
            pltpu.VMEM((H, C), bf16),
            pltpu.VMEM((C, C), bf16),
            pltpu.VMEM((1, C), f32),
            pltpu.VMEM((C, C), bf16),
            pltpu.VMEM((1, C), f32),
            pltpu.VMEM(blocks.shape, bf16),
            pltpu.VMEM(blocks.shape, bf16),
            pltpu.VMEM(blocks.shape, bf16),
            pltpu.VMEM((NY, NZ, NCORE, H * ROWS, RES), bf16),
            pltpu.VMEM((H, RES, RES), f32),
            pltpu.VMEM((3 * C, C), bf16),
            pltpu.VMEM((C, C), f32),
            pltpu.SemaphoreType.DMA((11,)),
            pltpu.SemaphoreType.DMA((CHUNKS,)),
            pltpu.SemaphoreType.DMA((CHUNKS,)),
            pltpu.SemaphoreType.DMA((CHUNKS,)),
            pltpu.SemaphoreType.DMA((CHUNKS,)),
            pltpu.SemaphoreType.DMA((10,)),
            pltpu.SemaphoreType.DMA((4,)),
        ],
        compiler_params=pltpu.CompilerParams(
            collective_id=0, has_side_effects=True, vmem_limit_bytes=60 * 2**20
        ),
    )(
        x, gain.reshape(1, C), shift.reshape(1, C), wq, wk, wv, wb.T, wg, gb.reshape(1, C), wo, ob.reshape(1, C)
    )
    return jnp.swapaxes(out.reshape(RES, ROWS, C), 0, 1)


def solution(mesh):
    return jax.shard_map(
        on_device,
        mesh=mesh,
        in_specs=(P(("dp", "axial"), None, None), P(), P(), P(), P(), P(), P(), P(), P(), P(), P()),
        out_specs=P(("dp", "axial"), None, None),
        check_vma=False,
    )
```

time: 97.7 us -> 51 us (0.52)
  blocking collectives: 66.6 us -> 0 us
  Pallas kernels: 0 us -> 48.9 us
  starting transfers between devices: 12.8 us -> 0 us
  matrix products: 8.01 us -> 0 us
  other arithmetic: 7.29 us -> 0 us
    pallas_call x0 -> x1, Pallas kernels: none -> 48.9 us  [on_device(): pl.pallas_call(kernel, out_shape=blocks, in_specs=[pl.BlockSpec(memory_sp...]
    all_gather x1 -> x0, blocking collectives: 45.6 us -> none  [on_device(): bias_whole = lax.all_gather(bias_rows, 'axial', axis=0, tiled=True)]
    all_to_all x1 -> x0, blocking collectives: 21 us -> none  [on_device(): lax.all_to_all(update_cols, 'axial', split_axis=0, concat_axis=1, tiled=T...]
    all_to_all x1 -> x0, starting transfers between devices: 12.8 us -> none  [on_device(): lax.all_to_all(normed, 'axial', split_axis=1, concat_axis=0, tiled=True)]
    dot_general x7 -> x0, matrix products: 8.01 us -> none  [the longest x1 3.46 us: bias_layout(): jnp.einsum('kic,ch->khi', normed, w_bias, preferred_element_type=jnp.floa...]
    reduce_sum x3 -> x0, other arithmetic: 4.74 us -> none  [the longest x1 1.74 us: normalize(): spread = jnp.mean((values_f - average) ** 2, axis=-1, keepdims=True)]
    convert_element_type x1 -> x0, other arithmetic: 2.38 us -> none  [normalize(): return scaled.astype(jnp.bfloat16)]
    reshape x1, local copies, waits for them, and re-layouts: 0.32 us -> 1.9 us  [on_device(): return jnp.swapaxes(out.reshape(RES, ROWS, C), 0, 1)]
  transfers between devices with their start and end apart: 1 -> 0, of which waited for: 0 -> 0; matrix products, arithmetic and copies ran while one was open for 4% -> 0% of each run, Pallas kernels for 0% -> 0%
where the time goes in v1:
time: 51 us; the launch traced here: 50.9 us
  Pallas kernels  48.9 us (96%)
  local copies, waits for them, and re-layouts  1.9 us (4%)
    pallas_call x1, Pallas kernels, on_device(): pl.pallas_call(kernel, out_shape=blocks, in_specs=[pl.BlockSpec(memory_sp...  48.9 us
    reshape x1, local copies, waits for them, and re-layouts, on_device(): return jnp.swapaxes(out.reshape(RES, ROWS, C), 0, 1)  1.9 us

profile of v1, /device:TPU:1, one launch (start us, length us, event | category | flops | bytes accessed | tf_op | source)
XLA Modules:
  0.0 50.9 jit_solution(2785933161931209217)
XLA Ops:
  0.0 48.9 %shard_map.109 = bf16[64,32,128]{2,1,0:T(8,128)(2,1)} custom-call(bf16[8,256,128]{2,1,0:T(8,128)(2,1)} %x_hbm.1, f32[1,128]{1,0:T(1,128)} %bitcast.11, f32[1,128]{1,0:T(1,128)} %bitcast.12, bf16[128,128]{1,0:T(8,128)(2,1)} %wq_hbm.1, bf16[128,128]{1,0:T(8,128)(2,1)} %wk_hbm.1, bf16[128,128]{1,0:T(8,128)(2,1)} %wv_hbm.1, bf16[4,128]{1,0:T(4,128)(2,1)} %bitcast.10, ...), custom_call_target="tpu_custom_call" | custom-call | tf_op jit(solution)/shard_map/pallas_call | solution.py:193
  48.9 1.9 %copy.14 = bf16[256,8,128]{2,0,1:T(8,128)(2,1)} copy(bf16[256,8,128]{2,1,0:T(8,128)(2,1)} %bitcast.9) | data formatting | bytes 1048576 | tf_op jit(solution)/shard_map/reshape | solution.py:231

commit v2 on v1

v2 whole, which is shorter than its diff:
```python
import functools

import jax
import jax.numpy as jnp
from jax import lax
from jax.experimental import pallas as pl
from jax.experimental.pallas import tpu as pltpu
from jax.sharding import PartitionSpec as P

MESH = pl.DeviceIdType.MESH
NZ, NY, NCORE = 8, 2, 2
N = NZ * NY * NCORE
ROWS = 8
RES = 256
C = 128
H = 4
DH = 32
CHUNKS = 4
COLS = RES // N // CHUNKS
MSG = COLS * ROWS

OFFSETS = [(dz, dy, dc) for dz in range(NZ) for dy in range(NY) for dc in range(NCORE)][1:]

NT = (((1,), (1,)), ((), ()))


def dot_nt(a, b):
    return lax.dot_general(a, b, NT, preferred_element_type=jnp.float32)


def dot_nn(a, b):
    return jnp.dot(a, b, preferred_element_type=jnp.float32)


def kernel(
    x_hbm, gain_hbm, offset_hbm, wq_hbm, wk_hbm, wv_hbm, wb_hbm, wg_hbm, gb_hbm, wo_hbm, ob_hbm,
    out_ref,
    x_v, gain_v, offset_v, wb_v, w_all, gb_v, wo_v, ob_v,
    send1, recv1, send2, bias_all, bias_f,
    load_sem, s1_sem, r1_sem, s2_sem, r2_sem, bs_sem, bz_sem, by_sem, bc_sem,
):
    me = lax.axis_index("axial")
    my_y, my_z, my_c = me // (NZ * NCORE), (me // NCORE) % NZ, me % NCORE

    def other(dz, dy, dc):
        return ((my_y + dy) % NY) * (NZ * NCORE) + ((my_z + dz) % NZ) * NCORE + (my_c + dc) % NCORE

    loads = []
    for n, (src, dst) in enumerate(
        [
            (x_hbm, x_v), (gain_hbm, gain_v), (offset_hbm, offset_v), (wb_hbm, wb_v),
            (wq_hbm, w_all.at[:, 0:C]), (wk_hbm, w_all.at[:, C : 2 * C]),
            (wv_hbm, w_all.at[:, 2 * C : 3 * C]), (wg_hbm, w_all.at[:, 3 * C : 4 * C]), (gb_hbm, gb_v), (wo_hbm, wo_v), (ob_hbm, ob_v),
        ]
    ):
        copy = pltpu.make_async_copy(src, dst, load_sem.at[n])
        copy.start()
        loads.append(copy)

    barrier = pltpu.get_barrier_semaphore()
    for off in OFFSETS:
        pl.semaphore_signal(barrier, inc=1, device_id={"axial": other(*off)}, device_id_type=MESH)

    for n in range(4):
        loads[n].wait()

    gain = gain_v[...][None]
    shift = offset_v[...][None]
    wb = wb_v[...].astype(jnp.float32)
    wb_rep = jnp.broadcast_to(wb[:, None, :], (H, ROWS, C)).reshape(H * ROWS, C)
    row_of = lax.broadcasted_iota(jnp.int32, (H * ROWS, C), 0) % ROWS
    wb_row = [jnp.where(row_of == r, wb_rep, 0.0).astype(jnp.bfloat16) for r in range(ROWS)]

    STEP = 32
    for block in range(RES // STEP):
        values = x_v[:, pl.ds(block * STEP, STEP), :].astype(jnp.float32)
        average = jnp.mean(values, axis=-1, keepdims=True)
        centred = values - average
        spread = jnp.mean(centred * centred, axis=-1, keepdims=True)
        scaled = centred * lax.rsqrt(spread + 1e-05) * gain + shift
        turned = jnp.swapaxes(scaled, 0, 1).reshape(STEP // 2, 2 * ROWS, C)
        turned = turned.astype(jnp.bfloat16).reshape(STEP * ROWS // MSG, MSG, C)
        first = block * STEP * ROWS // MSG
        send1[pl.ds(first, STEP * ROWS // MSG)] = turned
        x_v[:, pl.ds(block * STEP, STEP), :] = scaled.astype(jnp.bfloat16)

    acc = dot_nt(wb_row[0], x_v[0])
    for r in range(1, ROWS):
        acc = acc + dot_nt(wb_row[r], x_v[r])
    bias_all[me] = acc.astype(jnp.bfloat16)

    pl.semaphore_wait(barrier, N - 1)

    def bias_send(slot, sem, off):
        block = bias_all.at[slot]
        pltpu.make_async_remote_copy(
            src_ref=block, dst_ref=block, send_sem=bs_sem.at[0], recv_sem=sem,
            device_id={"axial": other(*off)}, device_id_type=MESH,
        ).start()

    def bias_wait(sem, count=1):
        blocks = bias_all.at[pl.ds(0, count)]
        pltpu.make_async_copy(blocks, blocks, sem).wait()

    def slot_of(dz, dy, dc=0):
        return other(NZ - dz, dy, dc)

    for dz in (4, 3, 5, 2, 6, 1, 7):
        bias_send(me, bz_sem.at[dz], (dz, 0, 0))
    bias_send(me, by_sem.at[0], (0, 1, 0))
    bias_send(me, bc_sem.at[0], (0, 0, 1))

    def exchange(c, src, dst, send_sem, recv_sem):
        for off in OFFSETS:
            to = other(*off)
            pltpu.make_async_remote_copy(
                src_ref=src.at[c * N + to], dst_ref=dst.at[c * N + me], send_sem=send_sem.at[c], recv_sem=recv_sem.at[c],
                device_id={"axial": to}, device_id_type=MESH,
            ).start()
        dst[c * N + me] = src[c * N + me]

    def arrived(c, ref, sem):
        part = ref.at[pl.ds(c * N, N - 1)]
        pltpu.make_async_copy(part, part, sem.at[c]).wait()

    for c in range(CHUNKS):
        exchange(c, send1, recv1, s1_sem, r1_sem)

    for step in ("z1", "z7", "y0", "z2", "z6", "y1", "y7", "z3", "z5", "y2", "y6", "z4", "y3", "y5"):
        dz = int(step[1])
        if step[0] == "z":
            bias_wait(bz_sem.at[dz])
            bias_send(slot_of(dz, 0), by_sem.at[dz], (0, 1, 0))
            bias_send(slot_of(dz, 0), bc_sem.at[0], (0, 0, 1))
        else:
            bias_wait(by_sem.at[dz])
            bias_send(slot_of(dz, 1), bc_sem.at[1], (0, 0, 1))

    def bias_half(y):
        lanes = pl.ds(pl.multiple_of(y * (RES // NY), RES // NY), RES // NY)
        slots = pl.ds(y * NZ * NCORE, NZ * NCORE)
        for h in range(H):
            part = bias_all[slots, h * ROWS : (h + 1) * ROWS, :]
            bias_f[h, :, lanes] = part.astype(jnp.float32).reshape(RES // NY, RES).T

    bias_wait(bc_sem.at[0], NZ)
    bias_half(my_y)
    bias_wait(by_sem.at[4])
    bias_send(slot_of(4, 1), bc_sem.at[1], (0, 0, 1))
    for n in range(4, len(loads)):
        loads[n].wait()
    bias_wait(bc_sem.at[1], NZ)
    bias_half(1 - my_y)

    lane_head = lax.broadcasted_iota(jnp.int32, (RES, C), 1) // DH
    scale = 1.0 / DH**0.5

    def attend(projected):
        queries = projected[:, 0:C] * scale
        keys = projected[:, C : 2 * C].astype(jnp.bfloat16)
        values = projected[:, 2 * C : 3 * C].astype(jnp.bfloat16)
        gating = jax.nn.sigmoid(projected[:, 3 * C :] + gb_v[...])
        for h in range(H):
            own = lane_head == h
            query_h = jnp.where(own, queries, 0.0).astype(jnp.bfloat16)
            scores = dot_nt(query_h, keys) + bias_f[h]
            expo = jnp.exp(scores - jnp.max(scores, axis=1, keepdims=True))
            total = jnp.broadcast_to(jnp.sum(expo, axis=1, keepdims=True), (RES, C))
            part = dot_nn(expo.astype(jnp.bfloat16), values)
            summed = part if h == 0 else jnp.where(own, part, summed)
            totals = total if h == 0 else jnp.where(own, total, totals)
        return (gating * (summed / totals)).astype(jnp.bfloat16)

    for c in range(CHUNKS):
        arrived(c, recv1, r1_sem)
        block = recv1[pl.ds(c * N, N)].astype(jnp.float32).reshape(N, COLS, ROWS, C)
        columns = jnp.concatenate([block[:, q].reshape(RES, C) for q in range(COLS)], axis=0).astype(jnp.bfloat16)
        projected = dot_nn(columns, w_all[...])
        gated = jnp.concatenate([attend(projected[q * RES : (q + 1) * RES]) for q in range(COLS)], axis=0)
        update = dot_nn(gated, wo_v[...]) + ob_v[...]
        parts = [update[q * RES : (q + 1) * RES].reshape(N, ROWS, C) for q in range(COLS)]
        send2[pl.ds(c * N, N)] = jnp.concatenate(parts, axis=1).astype(jnp.bfloat16)
        exchange(c, send2, out_ref, s2_sem, r2_sem)

    for c in range(CHUNKS):
        arrived(c, out_ref, r2_sem)
    bias_wait(bs_sem.at[0], NZ - 1 + 3 * NZ)
    for c in range(CHUNKS):
        arrived(c, send1, s1_sem)
        arrived(c, send2, s2_sem)


def on_device(x, gain, shift, wq, wk, wv, wb, wg, gb, wo, ob):
    blocks = jax.ShapeDtypeStruct((CHUNKS * N, MSG, C), jnp.bfloat16)
    bf16, f32 = jnp.bfloat16, jnp.float32
    out = pl.pallas_call(
        kernel,
        out_shape=blocks,
        in_specs=[pl.BlockSpec(memory_space=pltpu.HBM)] * 11,
        out_specs=pl.BlockSpec(memory_space=pltpu.VMEM),
        scratch_shapes=[
            pltpu.VMEM((ROWS, RES, C), bf16),
            pltpu.VMEM((1, C), f32),
            pltpu.VMEM((1, C), f32),
            pltpu.VMEM((H, C), bf16),
            pltpu.VMEM((C, 4 * C), bf16),
            pltpu.VMEM((1, C), f32),
            pltpu.VMEM((C, C), bf16),
            pltpu.VMEM((1, C), f32),
            pltpu.VMEM(blocks.shape, bf16),
            pltpu.VMEM(blocks.shape, bf16),
            pltpu.VMEM(blocks.shape, bf16),
            pltpu.VMEM((N, H * ROWS, RES), bf16),
            pltpu.VMEM((H, RES, RES), f32),
            pltpu.SemaphoreType.DMA((11,)),
            pltpu.SemaphoreType.DMA((CHUNKS,)),
            pltpu.SemaphoreType.DMA((CHUNKS,)),
            pltpu.SemaphoreType.DMA((CHUNKS,)),
            pltpu.SemaphoreType.DMA((CHUNKS,)),
            pltpu.SemaphoreType.DMA((1,)),
            pltpu.SemaphoreType.DMA((NZ,)),
            pltpu.SemaphoreType.DMA((NZ,)),
            pltpu.SemaphoreType.DMA((NCORE,)),
        ],
        compiler_params=pltpu.CompilerParams(
            collective_id=0, has_side_effects=True, vmem_limit_bytes=40 * 2**20
        ),
    )(
        *[pltpu.with_memory_space_constraint(a, pltpu.HBM) for a in (x, gain.reshape(1, C), shift.reshape(1, C), wq, wk, wv, wb.T, wg, gb.reshape(1, C), wo, ob.reshape(1, C))]
    )
    return jnp.swapaxes(out.reshape(RES, ROWS, C), 0, 1)


def solution(mesh):
    return jax.shard_map(
        on_device,
        mesh=mesh,
        in_specs=(P(("dp", "axial"), None, None), P(), P(), P(), P(), P(), P(), P(), P(), P(), P()),
        out_specs=P(("dp", "axial"), None, None),
        check_vma=False,
    )
```

time: 51 us -> 44.4 us (0.87)
  Pallas kernels: 48.9 us -> 43.4 us
  local copies, waits for them, and re-layouts: 1.9 us -> 0.88 us
    pallas_call x1, Pallas kernels: 48.9 us -> 43.4 us  [on_device(): pl.pallas_call(kernel, out_shape=blocks, in_specs=[pl.BlockSpec(memory_sp...]
    reshape x1, local copies, waits for them, and re-layouts: 1.9 us -> 0.88 us  [on_device(): return jnp.swapaxes(out.reshape(RES, ROWS, C), 0, 1)]
where the time goes in v2:
time: 44.4 us; the launch traced here: 44.3 us
  Pallas kernels  43.4 us (98%)
  local copies, waits for them, and re-layouts  0.88 us (2%)
    pallas_call x1, Pallas kernels, on_device(): pl.pallas_call(kernel, out_shape=blocks, in_specs=[pl.BlockSpec(memory_sp...  43.4 us

profile of v2, /device:TPU:1, one launch (start us, length us, event | category | flops | bytes accessed | tf_op | source)
XLA Modules:
  0.0 44.3 jit_solution(11878890606037356987)
XLA Ops:
  0.0 43.4 %shard_map.109 = bf16[128,16,128]{2,1,0:T(8,128)(2,1)S(1)} custom-call(bf16[8,256,128]{2,1,0:T(8,128)(2,1)} %x_hbm.1, f32[1,128]{1,0:T(1,128)} %bitcast.11, f32[1,128]{1,0:T(1,128)} %bitcast.12, bf16[128,128]{1,0:T(8,128)(2,1)} %wq_hbm.1, bf16[128,128]{1,0:T(8,128)(2,1)} %wk_hbm.1, bf16[128,128]{1,0:T(8,128)(2,1)} %wv_hbm.1, bf16[4,128]{1,0:T(4,128)(2,1)} %bitcast.10, ...), custom_call_target="tpu_custom_call" | custom-call | tf_op jit(solution)/shard_map/pallas_call | solution.py:196
  43.4 0.9 %copy.14 = bf16[256,8,128]{2,0,1:T(8,128)(2,1)} copy(bf16[256,8,128]{2,1,0:T(8,128)(2,1)S(1)} %bitcast.9) | data formatting | bytes 1048576 | tf_op jit(solution)/shard_map/reshape | solution.py:231

commit v3 on v2

--- a/solution.py
+++ b/solution.py
@@ -19,7 +19,7 @@
 COLS = RES // N // CHUNKS
 MSG = COLS * ROWS
 
-OFFSETS = [(dz, dy, dc) for dz in range(NZ) for dy in range(NY) for dc in range(NCORE)][1:]
+OFFSETS = [(dz, dy, dc) for dz in (4, 3, 5, 2, 6, 1, 7, 0) for dy in (1, 0) for dc in range(NCORE)][:-2] + [(0, 0, 1)]
 
 NT = (((1,), (1,)), ((), ()))
 
@@ -110,31 +110,36 @@
     bias_send(me, by_sem.at[0], (0, 1, 0))
     bias_send(me, bc_sem.at[0], (0, 0, 1))
 
-    def exchange(c, src, dst, send_sem, recv_sem):
-        for off in OFFSETS:
+    def exchange(c, src, dst, send_sem, recv_sem, offsets=OFFSETS):
+        for off in offsets:
             to = other(*off)
             pltpu.make_async_remote_copy(
                 src_ref=src.at[c * N + to], dst_ref=dst.at[c * N + me], send_sem=send_sem.at[c], recv_sem=recv_sem.at[c],
                 device_id={"axial": to}, device_id_type=MESH,
             ).start()
+
+    def keep(c, src, dst):
         dst[c * N + me] = src[c * N + me]
 
     def arrived(c, ref, sem):
         part = ref.at[pl.ds(c * N, N - 1)]
         pltpu.make_async_copy(part, part, sem.at[c]).wait()
 
-    for c in range(CHUNKS):
+    for c in range(2):
+        exchange(c, send1, recv1, s1_sem, r1_sem, [off for off in OFFSETS if off[1] == 0])
+    for dz in (1, 7, 2, 6, 3, 5, 4):
+        bias_wait(bz_sem.at[dz])
+        bias_send(slot_of(dz, 0), by_sem.at[dz], (0, 1, 0))
+        bias_send(slot_of(dz, 0), bc_sem.at[0], (0, 0, 1))
+    for c in range(2):
+        exchange(c, send1, recv1, s1_sem, r1_sem, [off for off in OFFSETS if off[1] == 1])
+    for c in range(2, CHUNKS):
         exchange(c, send1, recv1, s1_sem, r1_sem)
-
-    for step in ("z1", "z7", "y0", "z2", "z6", "y1", "y7", "z3", "z5", "y2", "y6", "z4", "y3", "y5"):
-        dz = int(step[1])
-        if step[0] == "z":
-            bias_wait(bz_sem.at[dz])
-            bias_send(slot_of(dz, 0), by_sem.at[dz], (0, 1, 0))
-            bias_send(slot_of(dz, 0), bc_sem.at[0], (0, 0, 1))
-        else:
-            bias_wait(by_sem.at[dz])
-            bias_send(slot_of(dz, 1), bc_sem.at[1], (0, 0, 1))
+    for c in range(CHUNKS):
+        keep(c, send1, recv1)
+    for dz in (0, 1, 7, 2, 6):
+        bias_wait(by_sem.at[dz])
+        bias_send(slot_of(dz, 1), bc_sem.at[1], (0, 0, 1))
 
     def bias_half(y):
         lanes = pl.ds(pl.multiple_of(y * (RES // NY), RES // NY), RES // NY)
@@ -145,8 +150,9 @@
 
     bias_wait(bc_sem.at[0], NZ)
     bias_half(my_y)
-    bias_wait(by_sem.at[4])
-    bias_send(slot_of(4, 1), bc_sem.at[1], (0, 0, 1))
+    for dz in (3, 5, 4):
+        bias_wait(by_sem.at[dz])
+        bias_send(slot_of(dz, 1), bc_sem.at[1], (0, 0, 1))
     for n in range(4, len(loads)):
         loads[n].wait()
     bias_wait(bc_sem.at[1], NZ)
@@ -180,7 +186,19 @@
         update = dot_nn(gated, wo_v[...]) + ob_v[...]
         parts = [update[q * RES : (q + 1) * RES].reshape(N, ROWS, C) for q in range(COLS)]
         send2[pl.ds(c * N, N)] = jnp.concatenate(parts, axis=1).astype(jnp.bfloat16)
-        exchange(c, send2, out_ref, s2_sem, r2_sem)
+        for z in (0, 1, 2, 3, 7, 4, 6, 5):
+            for y in range(NY):
+                for core in range(NCORE):
+                    to = y * NZ * NCORE + z * NCORE + core
+
+                    @pl.when(to != me)
+                    def _(to=to, c=c):
+                        pltpu.make_async_remote_copy(
+                            src_ref=send2.at[c * N + to], dst_ref=out_ref.at[c * N + me], send_sem=s2_sem.at[c],
+                            recv_sem=r2_sem.at[c], device_id={"axial": to}, device_id_type=MESH,
+                        ).start()
+
+        keep(c, send2, out_ref)
 
     for c in range(CHUNKS):
         arrived(c, out_ref, r2_sem)

time: 44.4 us -> 40.3 us (0.908)
  Pallas kernels: 43.4 us -> 39.3 us
    pallas_call x1, Pallas kernels: 43.4 us -> 39.3 us  [on_device(): pl.pallas_call(kernel, out_shape=blocks, in_specs=[pl.BlockSpec(memory_sp...]
where the time goes in v3:
time: 40.3 us; the launch traced here: 40.2 us
  Pallas kernels  39.3 us (98%)
  local copies, waits for them, and re-layouts  0.88 us (2%)
    pallas_call x1, Pallas kernels, on_device(): pl.pallas_call(kernel, out_shape=blocks, in_specs=[pl.BlockSpec(memory_sp...  39.3 us
    reshape x1, local copies, waits for them, and re-layouts, on_device(): return jnp.swapaxes(out.reshape(RES, ROWS, C), 0, 1)  0.88 us

profile of v3, /device:TPU:1, one launch (start us, length us, event | category | flops | bytes accessed | tf_op | source)
XLA Modules:
  0.0 40.2 jit_solution(17526267437827489364)
XLA Ops:
  0.0 39.3 %shard_map.109 = bf16[128,16,128]{2,1,0:T(8,128)(2,1)S(1)} custom-call(bf16[8,256,128]{2,1,0:T(8,128)(2,1)} %x_hbm.1, f32[1,128]{1,0:T(1,128)} %bitcast.11, f32[1,128]{1,0:T(1,128)} %bitcast.12, bf16[128,128]{1,0:T(8,128)(2,1)} %wq_hbm.1, bf16[128,128]{1,0:T(8,128)(2,1)} %wk_hbm.1, bf16[128,128]{1,0:T(8,128)(2,1)} %wv_hbm.1, bf16[4,128]{1,0:T(4,128)(2,1)} %bitcast.10, ...), custom_call_target="tpu_custom_call" | custom-call | tf_op jit(solution)/shard_map/pallas_call | solution.py:214
  39.3 0.9 %copy.14 = bf16[256,8,128]{2,0,1:T(8,128)(2,1)} copy(bf16[256,8,128]{2,1,0:T(8,128)(2,1)S(1)} %bitcast.9) | data formatting | bytes 1048576 | tf_op jit(solution)/shard_map/reshape | solution.py:249

commit v4 on v3

--- a/solution.py
+++ b/solution.py
@@ -36,7 +36,7 @@
     x_hbm, gain_hbm, offset_hbm, wq_hbm, wk_hbm, wv_hbm, wb_hbm, wg_hbm, gb_hbm, wo_hbm, ob_hbm,
     out_ref,
     x_v, gain_v, offset_v, wb_v, w_all, gb_v, wo_v, ob_v,
-    send1, recv1, send2, bias_all, bias_f,
+    send1, recv1, send2, got, bias_all, bias_f,
     load_sem, s1_sem, r1_sem, s2_sem, r2_sem, bs_sem, bz_sem, by_sem, bc_sem,
 ):
     me = lax.axis_index("axial")
@@ -125,15 +125,15 @@
         part = ref.at[pl.ds(c * N, N - 1)]
         pltpu.make_async_copy(part, part, sem.at[c]).wait()
 
-    for c in range(2):
+    for c in range(1):
         exchange(c, send1, recv1, s1_sem, r1_sem, [off for off in OFFSETS if off[1] == 0])
     for dz in (1, 7, 2, 6, 3, 5, 4):
         bias_wait(bz_sem.at[dz])
         bias_send(slot_of(dz, 0), by_sem.at[dz], (0, 1, 0))
         bias_send(slot_of(dz, 0), bc_sem.at[0], (0, 0, 1))
-    for c in range(2):
+    for c in range(1):
         exchange(c, send1, recv1, s1_sem, r1_sem, [off for off in OFFSETS if off[1] == 1])
-    for c in range(2, CHUNKS):
+    for c in range(1, CHUNKS):
         exchange(c, send1, recv1, s1_sem, r1_sem)
     for c in range(CHUNKS):
         keep(c, send1, recv1)
@@ -155,8 +155,6 @@
         bias_send(slot_of(dz, 1), bc_sem.at[1], (0, 0, 1))
     for n in range(4, len(loads)):
         loads[n].wait()
-    bias_wait(bc_sem.at[1], NZ)
-    bias_half(1 - my_y)
 
     lane_head = lax.broadcasted_iota(jnp.int32, (RES, C), 1) // DH
     scale = 1.0 / DH**0.5
@@ -182,6 +180,9 @@
         block = recv1[pl.ds(c * N, N)].astype(jnp.float32).reshape(N, COLS, ROWS, C)
         columns = jnp.concatenate([block[:, q].reshape(RES, C) for q in range(COLS)], axis=0).astype(jnp.bfloat16)
         projected = dot_nn(columns, w_all[...])
+        if c == 0:
+            bias_wait(bc_sem.at[1], NZ)
+            bias_half(1 - my_y)
         gated = jnp.concatenate([attend(projected[q * RES : (q + 1) * RES]) for q in range(COLS)], axis=0)
         update = dot_nn(gated, wo_v[...]) + ob_v[...]
         parts = [update[q * RES : (q + 1) * RES].reshape(N, ROWS, C) for q in range(COLS)]
@@ -194,14 +195,16 @@
                     @pl.when(to != me)
                     def _(to=to, c=c):
                         pltpu.make_async_remote_copy(
-                            src_ref=send2.at[c * N + to], dst_ref=out_ref.at[c * N + me], send_sem=s2_sem.at[c],
+                            src_ref=send2.at[c * N + to], dst_ref=got.at[c * N + me], send_sem=s2_sem.at[c],
                             recv_sem=r2_sem.at[c], device_id={"axial": to}, device_id_type=MESH,
                         ).start()
 
-        keep(c, send2, out_ref)
-
-    for c in range(CHUNKS):
-        arrived(c, out_ref, r2_sem)
+        keep(c, send2, got)
+
+    for c in range(CHUNKS):
+        arrived(c, got, r2_sem)
+        block = got[pl.ds(c * N, N)].astype(jnp.float32).reshape(N * COLS, ROWS, C)
+        out_ref[:, pl.ds(c * N * COLS, N * COLS), :] = jnp.swapaxes(block, 0, 1).astype(jnp.bfloat16)
     bias_wait(bs_sem.at[0], NZ - 1 + 3 * NZ)
     for c in range(CHUNKS):
         arrived(c, send1, s1_sem)
@@ -213,7 +216,7 @@
     bf16, f32 = jnp.bfloat16, jnp.float32
     out = pl.pallas_call(
         kernel,
-        out_shape=blocks,
+        out_shape=jax.ShapeDtypeStruct((ROWS, RES, C), bf16),
         in_specs=[pl.BlockSpec(memory_space=pltpu.HBM)] * 11,
         out_specs=pl.BlockSpec(memory_space=pltpu.VMEM),
         scratch_shapes=[
@@ -225,6 +228,7 @@
             pltpu.VMEM((1, C), f32),
             pltpu.VMEM((C, C), bf16),
             pltpu.VMEM((1, C), f32),
+            pltpu.VMEM(blocks.shape, bf16),
             pltpu.VMEM(blocks.shape, bf16),
             pltpu.VMEM(blocks.shape, bf16),
             pltpu.VMEM(blocks.shape, bf16),
@@ -246,7 +250,7 @@
     )(
         *[pltpu.with_memory_space_constraint(a, pltpu.HBM) for a in (x, gain.reshape(1, C), shift.reshape(1, C), wq, wk, wv, wb.T, wg, gb.reshape(1, C), wo, ob.reshape(1, C))]
     )
-    return jnp.swapaxes(out.reshape(RES, ROWS, C), 0, 1)
+    return out
 
 
 def solution(mesh):

time: 40.3 us -> 39.9 us (0.990)
    reshape x1 -> x0, local copies, waits for them, and re-layouts: 0.88 us -> none  [on_device(): return jnp.swapaxes(out.reshape(RES, ROWS, C), 0, 1)]
    unnamed x0 -> x1, local copies, waits for them, and re-layouts: none -> 0.8 us
where the time goes in v4:
time: 39.9 us; the launch traced here: 39.8 us
  Pallas kernels  39 us (98%)
  local copies, waits for them, and re-layouts  0.8 us (2%)
    pallas_call x1, Pallas kernels, on_device(): pl.pallas_call(kernel, out_shape=jax.ShapeDtypeStruct((ROWS, RES, C), bf1...  39 us

profile of v4, /device:TPU:1, one launch (start us, length us, event | category | flops | bytes accessed | tf_op | source)
XLA Modules:
  0.0 39.8 jit_solution(14934480843080633423)
XLA Ops:
  0.0 39.0 %shard_map.109 = bf16[8,256,128]{2,1,0:T(8,128)(2,1)S(1)} custom-call(bf16[8,256,128]{2,1,0:T(8,128)(2,1)} %x_hbm.1, f32[1,128]{1,0:T(1,128)} %bitcast.6, f32[1,128]{1,0:T(1,128)} %bitcast.7, bf16[128,128]{1,0:T(8,128)(2,1)} %wq_hbm.1, bf16[128,128]{1,0:T(8,128)(2,1)} %wk_hbm.1, bf16[128,128]{1,0:T(8,128)(2,1)} %wv_hbm.1, bf16[4,128]{1,0:T(4,128)(2,1)} %bitcast.5, ...), custom_call_target="tpu_custom_call" | custom-call | tf_op jit(solution)/shard_map/pallas_call | solution.py:217
  39.0 0.8 %copy.13 = bf16[8,256,128]{2,1,0:T(8,128)(2,1)} copy(bf16[8,256,128]{2,1,0:T(8,128)(2,1)S(1)} %shard_map.109) | data formatting | bytes 1048576
